TPU v7x, 32 devices: a whole 2x2x4 slice. The times are simulated.
32 devices in a mesh: wide: 8 (over z, y), narrow: 4 (over x, core).
Axes of the slice: x: 2, y: 2, z: 4, core: 2. Of those that a mesh axis runs over, the one named last changes fastest.
Arguments:
- slab: bfloat16 [6144, 2048], P('wide', 'narrow'), may hold values from -1.1953125 to 1.1953125
- occupation: float32 [4096], replicated, may hold values from 0.02 to 2
- column_band: int32 [2048], P('narrow'), may hold values from 0 to 4095
- pattern: int32 [48, 12], P('wide'), may hold values from 0 to 47, as said below
Outputs:
- density: bfloat16 [48, 12, 128, 128], P('wide', 'narrow')
Inputs may be any that keep to these rules, and one draw needn't show every extreme that they name: `pattern`: each row c lists 12 different clusters, each equal to (c + d) mod 48 with -8 <= d <= 8; d = -8 and d = 8 appear in every row.
All inputs are finite; a program needn't handle non-finite values.
Results may differ from a plain program's by a relative error of at most 0.015.
Values may be sent and summed in bfloat16 or wider, within the bound.
No kernel may reach another device: no remote copies, remote signals or barrier semaphores. Data moves between devices by JAX's collectives and lax.ppermute only.
A program may use at most 64 MiB of HBM per device.

v0:
```python
import functools

import jax
import jax.numpy as jnp
from jax import lax
from jax.experimental import pallas as pl
from jax.experimental.pallas import tpu as pltpu
from jax.sharding import PartitionSpec as P

B = 128
REACH = 8
CL = 6
PAIR = 2
VMEM = pl.BlockSpec(memory_space=pltpu.VMEM)
SMEM = pl.BlockSpec(memory_space=pltpu.SMEM)
LIMIT = 40 * 1024 * 1024
LONG = pl.CostEstimate(flops=20 * 10**9, bytes_accessed=1, transcendentals=0)
SHORT = pl.CostEstimate(flops=1, bytes_accessed=1, transcendentals=0)


def move(value, axis, target):
    count = lax.axis_size(axis)
    return lax.ppermute(value, axis, [(s, target(s) % count) for s in range(count)])


def outward(w):
    return w + 2 if w % 2 == 0 else w - 2


def natural(low, high):
    odd = lax.rem(lax.axis_index("wide"), 2)
    return jnp.where(odd == 1, low, CL - 1 - high)


def multiply(left, right):
    product = lax.dot_general(left, right, (((1,), (1,)), ((), ())), preferred_element_type=jnp.float32)
    return product.astype(jnp.bfloat16)


def add_pieces(marks, pieces, left, dense):
    for piece, mark in zip(pieces, marks):
        count = piece.shape[0] // B
        for at in range(0, count, PAIR):
            low, high = mark + at, mark + at + PAIR - 1
            c0, c1 = max(0, low - REACH), min(CL - 1, high + REACH)
            offset, start, rows = natural(low, high), natural(c0, c1), (c1 - c0 + 1) * B
            row = pl.multiple_of((offset - natural(mark, mark + count - 1)) * B, PAIR * B)
            product = multiply(
                left[pl.ds(pl.multiple_of(start * B, B), rows), :], piece[pl.ds(row, PAIR * B), :]
            )
            for r in range(c1 - c0 + 1):
                for h in range(PAIR):
                    dense[start + r, offset + REACH + h] = product[r * B : (r + 1) * B, h * B : (h + 1) * B]


def pieces_kernel(marks, left, *refs):
    add_pieces(marks, refs[: len(marks)], left, refs[-1])


def pieces_blocks(left, pieces, cost, dense=None):
    held = [] if dense is None else [dense]
    return pl.pallas_call(
        functools.partial(pieces_kernel, list(pieces)),
        out_shape=jax.ShapeDtypeStruct((CL, CL + 2 * REACH, B, B), jnp.bfloat16),
        in_specs=[VMEM] * (1 + len(pieces) + len(held)),
        out_specs=VMEM,
        input_output_aliases={1 + len(pieces): 0} if held else {},
        compiler_params=pltpu.CompilerParams(vmem_limit_bytes=LIMIT),
        cost_estimate=cost,
        name="pieces_blocks",
    )(left, *pieces.values(), *held)


def ends_kernel(weight, near, far, out):
    odd = lax.rem(lax.axis_index("wide"), 2) == 1
    left = (near[...].astype(jnp.float32) * weight[...]).astype(jnp.bfloat16)
    product = multiply(left, far[...])
    for at, (c, m) in enumerate(((-1, 6), (-1, 7), (-2, 6))):
        here, there = ((c + 2) * B, (m - 6) * B), ((-1 - c) * B, (7 - m) * B)
        one, two = [product[row : row + B, column : column + B] for row, column in (here, there)]
        out[at] = jnp.where(odd, one, two)


def end_blocks(weight, near, far):
    return pl.pallas_call(
        ends_kernel,
        out_shape=jax.ShapeDtypeStruct((3, B, B), jnp.bfloat16),
        in_specs=[VMEM] * 3,
        out_specs=VMEM,
        compiler_params=pltpu.CompilerParams(vmem_limit_bytes=LIMIT),
        cost_estimate=SHORT,
        name="end_blocks",
    )(weight[None, :], near, far)


def choose_kernel(share, marks, shares, ends, all_places, left, from_partner, after, *refs):
    dense = refs[len(marks) + 1]
    outs = refs[len(marks) + 2 : -2]
    places, done = refs[-2:]
    fetch = pltpu.make_async_copy(all_places, places, done)
    fetch.start()
    add_pieces(marks, refs[: len(marks)], left, dense)
    if ends:
        for at, (c, m) in enumerate(((0, -7), (0, -8), (1, -7))):
            dense[natural(c, c), natural(m, m) + REACH] = from_partner[at]
    fetch.wait()
    me = lax.axis_index("narrow")
    for out, (mask, (first, last)) in zip(outs, shares):
        start, slot0 = natural(first, last), (me ^ mask) * share
        for c in range(last - first + 1):
            for s in range(share):
                out[c, s] = dense[start + c, places[start + c, slot0 + s]]


def choose_blocks(share, shares, ends, places, left, from_partner, after, pieces, dense):
    shapes = [jax.ShapeDtypeStruct(dense.shape, dense.dtype)]
    shapes += [jax.ShapeDtypeStruct((last - first + 1, share, B, B), jnp.bfloat16) for _, (first, last) in shares]
    return pl.pallas_call(
        functools.partial(choose_kernel, share, list(pieces), shares, ends),
        out_shape=shapes,
        in_specs=[VMEM] * (5 + len(pieces)),
        out_specs=[VMEM] * len(shapes),
        scratch_shapes=[pltpu.SMEM(places.shape, places.dtype), pltpu.SemaphoreType.DMA],
        input_output_aliases={4 + len(pieces): 0},
        compiler_params=pltpu.CompilerParams(vmem_limit_bytes=LIMIT),
        cost_estimate=SHORT,
        name="choose_blocks",
    )(places, left, from_partner, after, *pieces.values(), dense)


def add_kernel(x, y, out):
    out[...] = (x[...].astype(jnp.float32) + y[...].astype(jnp.float32)).astype(jnp.bfloat16)


def add(x, y):
    return pl.pallas_call(
        add_kernel,
        out_shape=jax.ShapeDtypeStruct(x.shape, x.dtype),
        in_specs=[VMEM] * 2,
        out_specs=VMEM,
        compiler_params=pltpu.CompilerParams(vmem_limit_bytes=LIMIT),
        cost_estimate=SHORT,
        name="add",
    )(x, y)


def total_kernel(chunk, near, got, out):
    start = natural(*chunk)
    for r in range(out.shape[0]):
        out[r] = near[start + r].astype(jnp.float32) + got[r].astype(jnp.float32)


def total(chunk, near, got):
    return pl.pallas_call(
        functools.partial(total_kernel, chunk),
        out_shape=jax.ShapeDtypeStruct(got.shape, jnp.float32),
        in_specs=[VMEM] * 2,
        out_specs=VMEM,
        compiler_params=pltpu.CompilerParams(vmem_limit_bytes=LIMIT),
        cost_estimate=LONG,
        name="total",
    )(near, got)


def finish_kernel(chunks, early, near, got_near, got, out, rows, done):
    copies = []

    def write(row, total):
        at = len(copies)
        rows[at] = total.astype(jnp.bfloat16)
        copies.append(pltpu.make_async_copy(rows.at[at], out.at[row], done.at[at]))
        copies[-1].start()

    start, later = [natural(*chunk) for chunk in chunks]
    for r in range(early.shape[0]):
        write(start + r, early[r] + got_near[start + r].astype(jnp.float32))
    for r in range(got.shape[0]):
        total = near[later + r].astype(jnp.float32) + got_near[later + r].astype(jnp.float32)
        write(later + r, total + got[r].astype(jnp.float32))
    for copy in copies:
        copy.wait()


def finish(chunks, early, near, got_near, got):
    return pl.pallas_call(
        functools.partial(finish_kernel, chunks),
        out_shape=jax.ShapeDtypeStruct(near.shape, near.dtype),
        in_specs=[VMEM] * 4,
        out_specs=pl.BlockSpec(memory_space=pl.ANY),
        scratch_shapes=[pltpu.VMEM(near.shape, near.dtype), pltpu.SemaphoreType.DMA((CL,))],
        compiler_params=pltpu.CompilerParams(vmem_limit_bytes=LIMIT),
        cost_estimate=SHORT,
        name="finish",
    )(early, near, got_near, got)


def take_kernel(which, slab, *refs):
    out, done = refs[-2:]
    odd = lax.rem(lax.axis_index("wide"), 2)
    row = {"end": odd * 2, "middle": 1, "near": (1 - odd) * 2}[which] * PAIR * B
    copy = pltpu.make_async_copy(slab.at[pl.ds(pl.multiple_of(row, PAIR * B), PAIR * B), :], out, done)
    copy.start()
    copy.wait()


def take(slab, which, *after):
    return pl.pallas_call(
        functools.partial(take_kernel, which),
        out_shape=jax.ShapeDtypeStruct((PAIR * B, slab.shape[1]), slab.dtype),
        in_specs=[pl.BlockSpec(memory_space=pl.ANY)] + [VMEM] * len(after),
        out_specs=VMEM,
        scratch_shapes=[pltpu.SemaphoreType.DMA],
        compiler_params=pltpu.CompilerParams(vmem_limit_bytes=LIMIT),
        cost_estimate=SHORT,
        name=f"take_{which}",
    )(slab, *after)


def per_device(slab, occupation, column_band, pattern):
    clusters = CL * lax.axis_size("wide")
    share = pattern.shape[1] // lax.axis_size("narrow")
    odd = lax.axis_index("wide") % 2
    rows = PAIR * B
    partner = lambda w: w ^ 1

    places = jnp.mod(pattern - (lax.axis_index("wide") * CL - REACH), clusters)
    picks = column_band[:, None] == jnp.arange(occupation.shape[0], dtype=jnp.int32)[None, :]
    weight = jnp.sum(jnp.where(picks, occupation[None, :], jnp.float32(0.0)), axis=1)
    scaled = (slab.astype(jnp.float32) * weight[None, :]).astype(jnp.bfloat16)

    early = {0: slab}
    end_rows = take(slab, "end", jnp.zeros((8, 128), jnp.float32))
    middle_rows = take(slab, "middle", jnp.zeros((8, 128), jnp.float32))
    later_rows = take(slab, "near", end_rows)
    near_rows = take(slab, "near", later_rows, middle_rows)
    early[-6] = move(end_rows, "wide", partner)
    early[12] = move(later_rows, "wide", outward)
    early[-4] = move(middle_rows, "wide", partner)
    near = move(near_rows, "wide", partner)
    early[6] = move(early[-6], "wide", outward)
    early[8] = move(early[-4], "wide", outward)
    early[-2] = near
    late = {10: move(near, "wide", outward)}
    from_partner = move(end_blocks(weight, near, early[6]), "wide", partner)

    dense = pieces_blocks(scaled, early, LONG)
    chunks = ((0, 1), (2, 5))

    after = scaled
    sums = []
    for pieces, chunk, ends in (({}, chunks[0], True), (late, chunks[1], False)):
        dense, send, keep = choose_blocks(
            share, [(3, chunk), (2, chunk)], ends, places, scaled, from_partner, after, pieces, dense
        )
        after = move(send, "narrow", lambda n: n ^ 1)
        sums.append(move(add(keep, after), "narrow", lambda n: n ^ 2))
    everyone = (0, CL - 1)
    _, send, near = choose_blocks(
        share, [(1, everyone), (0, everyone)], False, places, scaled, from_partner, scaled, {}, dense
    )
    got_near = move(send, "narrow", lambda n: n ^ 1)
    return finish(chunks, total(chunks[0], near, sums[0]), near, got_near, sums[1])


def solution(mesh):
    placed = (P("wide", "narrow"), P(), P("narrow"), P("wide", None))
    return jax.shard_map(
        per_device,
        mesh=mesh,
        in_specs=placed,
        out_specs=P("wide", "narrow", None, None),
        check_vma=False,
    )
```

profile of v0, /device:TPU:0, one launch (start us, length us, event | category | flops | bytes accessed | tf_op | source)
XLA Modules:
  0.0 49.7 jit_solution(14473143218727295254)
XLA Ops:
  0.0 0.0 copy-start.2
  0.0 0.0 copy-start
  0.0 1.1 %copy-done = bf16[768,512]{1,0:T(8,128)(2,1)S(1)} copy-done((bf16[768,512]{1,0:T(8,128)(2,1)S(1)}, bf16[768,512]{1,0:T(8,128)(2,1)}, u32[]{:S(2)}) %copy-start) | copy-done | bytes 786456
  1.1 0.0 copy-start.3
  1.2 0.0 copy-start.4
  1.2 0.0 copy-start.1
  1.2 3.0 %collective-permute-start.1 = (bf16[256,512]{1,0:T(8,128)(2,1)S(1)}, bf16[256,512]{1,0:T(8,128)(2,1)S(1)}, u32[]{:S(2)}, u32[]{:S(2)}) collective-permute-start(bf16[256,512]{1,0:T(8,128)(2,1)S(1)} %take_end.1.refs_0_), channel_id=1, source_target_pairs={{0,4},{4,0},{8,12},{12,8},{16,20},{20,16},{24,28},{28,24},{1,5},{5... | collective-permute-start | bytes 786440 | tf_op jit(solution)/shard_map/ppermute | solution.py:23
  4.3 0.1 collective-permute-start.5
  4.4 2.1 %collective-permute-start.4 = (bf16[256,512]{1,0:T(8,128)(2,1)S(1)}, bf16[256,512]{1,0:T(8,128)(2,1)S(1)}, u32[]{:S(2)}, u32[]{:S(2)}) collective-permute-start(bf16[256,512]{1,0:T(8,128)(2,1)S(1)} %take_near.2.refs_0_), channel_id=1, source_target_pairs={{0,8},{4,28},{8,16},{12,4},{16,24},{20,12},{24,0},{28,20},{1,9},{5... | collective-permute-start | bytes 786440 | tf_op jit(solution)/shard_map/ppermute | solution.py:23
  6.5 3.6 %collective-permute-start = (bf16[256,512]{1,0:T(8,128)(2,1)S(1)}, bf16[256,512]{1,0:T(8,128)(2,1)S(1)}, u32[]{:S(2)}, u32[]{:S(2)}) collective-permute-start(bf16[256,512]{1,0:T(8,128)(2,1)S(1)} %take_near.3), channel_id=1, source_target_pairs={{0,4},{4,0},{8,12},{12,8},{16,20},{20,16},{24,28},{28,24},{1,5},{5... | collective-permute-start | bytes 786440 | tf_op jit(solution)/shard_map/ppermute | solution.py:23
  10.1 0.0 copy-done.3
  10.1 0.0 copy-done.4
  10.2 1.2 %select_reduce_fusion = f32[512]{0:T(512)S(1)} fusion(f32[4096]{0:T(1024)S(1)} %copy-done.3, s32[512]{0:T(512)S(1)} %copy-done.4), kind=kLoop, calls=%fused_computation | loop fusion | flops 6290944 | bytes 20480 | tf_op jit(solution)/shard_map/reduce_sum | solution.py:228
  11.4 0.0 copy-done.2
  11.4 0.0 collective-permute-done.1.refs_1_
  11.4 2.1 %collective-permute-start.2 = (bf16[256,512]{1,0:T(8,128)(2,1)S(1)}, bf16[256,512]{1,0:T(8,128)(2,1)S(1)}, u32[]{:S(2)}, u32[]{:S(2)}) collective-permute-start(bf16[256,512]{1,0:T(8,128)(2,1)S(1)} %collective-permute-done.1.refs_1_), channel_id=1, source_target_pairs={{0,8},{4,28},{8,16},{12,4},{16,24},{20,12},{24,0},{28,20},{1,9},{5... | collective-permute-start | bytes 786440 | tf_op jit(solution)/shard_map/ppermute | solution.py:23
  13.5 3.5 %collective-permute-done.5.refs_3_ = bf16[256,512]{1,0:T(8,128)(2,1)S(1)} collective-permute-done((bf16[256,512]{1,0:T(8,128)(2,1)S(1)}, bf16[256,512]{1,0:T(8,128)(2,1)S(1)}, u32[]{:S(2)}, u32[]{:S(2)}) %collective-permute-start.5) | collective-permute-done | bytes 262176 | tf_op jit(solution)/shard_map/ppermute | solution.py:23
  17.0 2.1 %collective-permute-start.6 = (bf16[256,512]{1,0:T(8,128)(2,1)S(1)}, bf16[256,512]{1,0:T(8,128)(2,1)S(1)}, u32[]{:S(2)}, u32[]{:S(2)}) collective-permute-start(bf16[256,512]{1,0:T(8,128)(2,1)S(1)} %collective-permute-done.5.refs_3_), channel_id=1, source_target_pairs={{0,8},{4,28},{8,16},{12,4},{16,24},{20,12},{24,0},{28,20},{1,9},{5... | collective-permute-start | bytes 786440 | tf_op jit(solution)/shard_map/ppermute | solution.py:23
  19.1 0.0 copy-done.1
  19.1 0.1 multiply_convert_fusion.left.after
  19.2 2.5 %collective-permute-done.near.refs_6_ = bf16[256,512]{1,0:T(8,128)(2,1)S(1)} collective-permute-done((bf16[256,512]{1,0:T(8,128)(2,1)S(1)}, bf16[256,512]{1,0:T(8,128)(2,1)S(1)}, u32[]{:S(2)}, u32[]{:S(2)}) %collective-permute-start) | collective-permute-done | bytes 262176 | tf_op jit(solution)/shard_map/ppermute | solution.py:23
  21.8 1.8 %collective-permute-start.8 = (bf16[256,512]{1,0:T(8,128)(2,1)S(1)}, bf16[256,512]{1,0:T(8,128)(2,1)S(1)}, u32[]{:S(2)}, u32[]{:S(2)}) collective-permute-start(bf16[256,512]{1,0:T(8,128)(2,1)S(1)} %collective-permute-done.near.refs_6_), channel_id=1, source_target_pairs={{0,8},{4,28},{8,16},{12,4},{16,24},{20,12},{24,0},{28,20},{1,9},{5... | collective-permute-start | bytes 786440 | tf_op jit(solution)/shard_map/ppermute | solution.py:23
  23.6 0.0 collective-permute-done.2.far.refs_4_
  23.6 0.3 end_blocks.1
  23.9 3.6 %collective-permute-start.3 = (bf16[3,128,128]{2,1,0:T(8,128)(2,1)S(1)}, bf16[3,128,128]{2,1,0:T(8,128)(2,1)S(1)}, u32[]{:S(2)}, u32[]{:S(2)}) collective-permute-start(bf16[3,128,128]{2,1,0:T(8,128)(2,1)S(1)} %end_blocks.1), channel_id=1, source_target_pairs={{0,4},{4,0},{8,12},{12,8},{16,20},{20,16},{24,28},{28,24},{1,5},{5... | collective-permute-start | bytes 294920 | tf_op jit(solution)/shard_map/ppermute | solution.py:23
  27.5 0.0 collective-permute-done.4.refs_2_
  27.5 0.0 collective-permute-done.6.refs_5_
  27.5 1.9 %pieces_blocks.1.refs_0_ = bf16[6,22,128,128]{3,2,1,0:T(8,128)(2,1)S(1)} custom-call(bf16[768,512]{1,0:T(8,128)(2,1)S(1)} %multiply_convert_fusion.left.after, bf16[768,512]{1,0:T(8,128)(2,1)S(1)} %copy-done.1, bf16[256,512]{1,0:T(8,128)(2,1)S(1)} %collective-permute-done.1.refs_1_, bf16[256,512]{1,0:T(8,128)(2,1)S(1)} %collective-permute-done.4.refs_2_, ...), custom_call_target="tpu_custom_call" | custom-call | flops 20000000000 | bytes 1 | tf_op jit(solution)/shard_map/pieces_blocks/pallas_call | solution.py:62
  29.3 0.7 %collective-permute-done.3.from_partner = bf16[3,128,128]{2,1,0:T(8,128)(2,1)S(1)} collective-permute-done((bf16[3,128,128]{2,1,0:T(8,128)(2,1)S(1)}, bf16[3,128,128]{2,1,0:T(8,128)(2,1)S(1)}, u32[]{:S(2)}, u32[]{:S(2)}) %collective-permute-start.3) | collective-permute-done | bytes 98336 | tf_op jit(solution)/shard_map/ppermute | solution.py:23
  30.1 0.6 %choose_blocks.3 = (bf16[6,22,128,128]{3,2,1,0:T(8,128)(2,1)S(1)}, bf16[2,3,128,128]{3,2,1,0:T(8,128)(2,1)S(1)}, bf16[2,3,128,128]{3,2,1,0:T(8,128)(2,1)S(1)}) custom-call(s32[6,12]{1,0:T(8,128)S(1)} %add_select_fusion.all_places, bf16[768,512]{1,0:T(8,128)(2,1)S(1)} %multiply_convert_fusion.left.after, ...), custom_call_target="tpu_custom_call", output_to_operand_aliasing={{0}: (4, {})} | custom-call | flops 1 | bytes 1 | tf_op jit(solution)/shard_map/choose_blocks/pallas_call | solution.py:118
  30.7 0.1 collective-permute-start.7
  30.8 0.7 %collective-permute-done.8.refs_0_ = bf16[256,512]{1,0:T(8,128)(2,1)S(1)} collective-permute-done((bf16[256,512]{1,0:T(8,128)(2,1)S(1)}, bf16[256,512]{1,0:T(8,128)(2,1)S(1)}, u32[]{:S(2)}, u32[]{:S(2)}) %collective-permute-start.8) | collective-permute-done | bytes 262176 | tf_op jit(solution)/shard_map/ppermute | solution.py:23
  31.4 0.8 %collective-permute-done.7.after.y = bf16[2,3,128,128]{3,2,1,0:T(8,128)(2,1)S(1)} collective-permute-done((bf16[2,3,128,128]{3,2,1,0:T(8,128)(2,1)S(1)}, bf16[2,3,128,128]{3,2,1,0:T(8,128)(2,1)S(1)}, u32[]{:S(2)}, u32[]{:S(2)}) %collective-permute-start.7) | collective-permute-done | bytes 196640 | tf_op jit(solution)/shard_map/ppermute | solution.py:23
  32.2 0.7 %choose_blocks.4 = (bf16[6,22,128,128]{3,2,1,0:T(8,128)(2,1)S(1)}, bf16[4,3,128,128]{3,2,1,0:T(8,128)(2,1)S(1)}, bf16[4,3,128,128]{3,2,1,0:T(8,128)(2,1)S(1)}) custom-call(s32[6,12]{1,0:T(8,128)S(1)} %add_select_fusion.all_places, bf16[768,512]{1,0:T(8,128)(2,1)S(1)} %multiply_convert_fusion.left.after, ...), custom_call_target="tpu_custom_call", output_to_operand_aliasing={{0}: (5, {})} | custom-call | flops 1 | bytes 1 | tf_op jit(solution)/shard_map/choose_blocks/pallas_call | solution.py:118
  32.9 0.2 collective-permute-start.11
  33.1 1.6 %collective-permute-start.9 = (bf16[2,3,128,128]{3,2,1,0:T(8,128)(2,1)S(1)}, bf16[2,3,128,128]{3,2,1,0:T(8,128)(2,1)S(1)}, u32[]{:S(2)}, u32[]{:S(2)}) collective-permute-start(bf16[2,3,128,128]{3,2,1,0:T(8,128)(2,1)S(1)} %add.11), channel_id=1, source_target_pairs={{0,2},{1,3},{2,0},{3,1},{4,6},{5,7},{6,4},{7,5},{8,10},{9,11},{10,... | collective-permute-start | bytes 589832 | tf_op jit(solution)/shard_map/ppermute | solution.py:23
  34.7 0.7 %choose_blocks.5 = (bf16[6,22,128,128]{3,2,1,0:T(8,128)(2,1)S(1)}, bf16[6,3,128,128]{3,2,1,0:T(8,128)(2,1)S(1)}, bf16[6,3,128,128]{3,2,1,0:T(8,128)(2,1)S(1)}) custom-call(s32[6,12]{1,0:T(8,128)S(1)} %add_select_fusion.all_places, bf16[768,512]{1,0:T(8,128)(2,1)S(1)} %multiply_convert_fusion.left.after, ...), custom_call_target="tpu_custom_call", output_to_operand_aliasing={{0}: (4, {})} | custom-call | flops 1 | bytes 1 | tf_op jit(solution)/shard_map/choose_blocks/pallas_call | solution.py:118
  35.4 0.1 collective-permute-start.10
  35.5 0.0 collective-permute-done.11.y
  35.5 0.1 add.12
  35.6 0.7 %collective-permute-start.12 = (bf16[4,3,128,128]{3,2,1,0:T(8,128)(2,1)S(1)}, bf16[4,3,128,128]{3,2,1,0:T(8,128)(2,1)S(1)}, u32[]{:S(2)}, u32[]{:S(2)}) collective-permute-start(bf16[4,3,128,128]{3,2,1,0:T(8,128)(2,1)S(1)} %add.12), channel_id=1, source_target_pairs={{0,2},{1,3},{2,0},{3,1},{4,6},{5,7},{6,4},{7,5},{8,10},{9,11},{10,... | collective-permute-start | bytes 1179656 | tf_op jit(solution)/shard_map/ppermute | solution.py:23
  36.3 4.6 %collective-permute-done.9.got = bf16[2,3,128,128]{3,2,1,0:T(8,128)(2,1)S(1)} collective-permute-done((bf16[2,3,128,128]{3,2,1,0:T(8,128)(2,1)S(1)}, bf16[2,3,128,128]{3,2,1,0:T(8,128)(2,1)S(1)}, u32[]{:S(2)}, u32[]{:S(2)}) %collective-permute-start.9) | collective-permute-done | bytes 196640 | tf_op jit(solution)/shard_map/ppermute | solution.py:23
  40.9 0.1 total.1.early
  41.0 0.0 collective-permute-done.10.got_near
  41.0 7.8 %collective-permute-done.12.got = bf16[4,3,128,128]{3,2,1,0:T(8,128)(2,1)S(1)} collective-permute-done((bf16[4,3,128,128]{3,2,1,0:T(8,128)(2,1)S(1)}, bf16[4,3,128,128]{3,2,1,0:T(8,128)(2,1)S(1)}, u32[]{:S(2)}, u32[]{:S(2)}) %collective-permute-start.12) | collective-permute-done | bytes 393248 | tf_op jit(solution)/shard_map/ppermute | solution.py:23
  48.8 0.9 %finish.1 = bf16[6,3,128,128]{3,2,1,0:T(8,128)(2,1)} custom-call(f32[2,3,128,128]{3,2,1,0:T(8,128)S(1)} %total.1.early, bf16[6,3,128,128]{3,2,1,0:T(8,128)(2,1)S(1)} %get-tuple-element.16.near, bf16[6,3,128,128]{3,2,1,0:T(8,128)(2,1)S(1)} %collective-permute-done.10.got_near, bf16[4,3,128,128]{3,2,1,0:T(8,128)(2,1)S(1)} %collective-permute-done.12.got), custom_call_target="tpu_custom_call" | custom-call | flops 1 | bytes 1 | tf_op jit(solution)/shard_map/finish/pallas_call | solution.py:185
  (7 shorter events, 0.2 us)
Async XLA Ops:
  0.0 11.4 %copy-start.2 = (s32[6,12]{1,0:T(8,128)S(1)}, s32[6,12]{1,0:T(8,128)}, u32[]{:S(2)}) copy-start(s32[6,12]{1,0:T(8,128)} %param.7) | copy-start | bytes 868
  0.0 1.1 %copy-start = (bf16[768,512]{1,0:T(8,128)(2,1)S(1)}, bf16[768,512]{1,0:T(8,128)(2,1)}, u32[]{:S(2)}) copy-start(bf16[768,512]{1,0:T(8,128)(2,1)} %refs_0_.1) | copy-start | bytes 2359300
  1.1 9.0 %copy-start.3 = (f32[4096]{0:T(1024)S(1)}, f32[4096]{0:T(1024)}, u32[]{:S(2)}) copy-start(f32[4096]{0:T(1024)} %param.5) | copy-start | bytes 49156
  1.2 9.0 %copy-start.4 = (s32[512]{0:T(512)S(1)}, s32[512]{0:T(512)}, u32[]{:S(2)}) copy-start(s32[512]{0:T(512)} %param.6) | copy-start | bytes 6148
  1.2 17.9 %copy-start.1 = (bf16[768,512]{1,0:T(8,128)(2,1)S(1)}, bf16[768,512]{1,0:T(8,128)(2,1)}, u32[]{:S(2)}) copy-start(bf16[768,512]{1,0:T(8,128)(2,1)} %refs_0_.1) | copy-start | bytes 2359300
  1.2 10.2 %collective-permute-start.1 = (bf16[256,512]{1,0:T(8,128)(2,1)S(1)}, bf16[256,512]{1,0:T(8,128)(2,1)S(1)}, u32[]{:S(2)}, u32[]{:S(2)}) collective-permute-start(bf16[256,512]{1,0:T(8,128)(2,1)S(1)} %take_end.1.refs_0_), channel_id=1, source_target_pairs={{0,4},{4,0},{8,12},{12,8},{16,20},{20,16},{24,28},{28,24},{1,5},{5... | collective-permute-start | bytes 786440 | tf_op jit(solution)/shard_map/ppermute | solution.py:23
  4.3 12.7 %collective-permute-start.5 = (bf16[256,512]{1,0:T(8,128)(2,1)S(1)}, bf16[256,512]{1,0:T(8,128)(2,1)S(1)}, u32[]{:S(2)}, u32[]{:S(2)}) collective-permute-start(bf16[256,512]{1,0:T(8,128)(2,1)S(1)} %take_middle.1.refs_1_), channel_id=1, source_target_pairs={{0,4},{4,0},{8,12},{12,8},{16,20},{20,16},{24,28},{28,24},{1,5},{5... | collective-permute-start | bytes 786440 | tf_op jit(solution)/shard_map/ppermute | solution.py:23
  4.4 23.1 %collective-permute-start.4 = (bf16[256,512]{1,0:T(8,128)(2,1)S(1)}, bf16[256,512]{1,0:T(8,128)(2,1)S(1)}, u32[]{:S(2)}, u32[]{:S(2)}) collective-permute-start(bf16[256,512]{1,0:T(8,128)(2,1)S(1)} %take_near.2.refs_0_), channel_id=1, source_target_pairs={{0,8},{4,28},{8,16},{12,4},{16,24},{20,12},{24,0},{28,20},{1,9},{5... | collective-permute-start | bytes 786440 | tf_op jit(solution)/shard_map/ppermute | solution.py:23
  6.5 15.2 %collective-permute-start = (bf16[256,512]{1,0:T(8,128)(2,1)S(1)}, bf16[256,512]{1,0:T(8,128)(2,1)S(1)}, u32[]{:S(2)}, u32[]{:S(2)}) collective-permute-start(bf16[256,512]{1,0:T(8,128)(2,1)S(1)} %take_near.3), channel_id=1, source_target_pairs={{0,4},{4,0},{8,12},{12,8},{16,20},{20,16},{24,28},{28,24},{1,5},{5... | collective-permute-start | bytes 786440 | tf_op jit(solution)/shard_map/ppermute | solution.py:23
  11.4 12.2 %collective-permute-start.2 = (bf16[256,512]{1,0:T(8,128)(2,1)S(1)}, bf16[256,512]{1,0:T(8,128)(2,1)S(1)}, u32[]{:S(2)}, u32[]{:S(2)}) collective-permute-start(bf16[256,512]{1,0:T(8,128)(2,1)S(1)} %collective-permute-done.1.refs_1_), channel_id=1, source_target_pairs={{0,8},{4,28},{8,16},{12,4},{16,24},{20,12},{24,0},{28,20},{1,9},{5... | collective-permute-start | bytes 786440 | tf_op jit(solution)/shard_map/ppermute | solution.py:23
  17.0 10.5 %collective-permute-start.6 = (bf16[256,512]{1,0:T(8,128)(2,1)S(1)}, bf16[256,512]{1,0:T(8,128)(2,1)S(1)}, u32[]{:S(2)}, u32[]{:S(2)}) collective-permute-start(bf16[256,512]{1,0:T(8,128)(2,1)S(1)} %collective-permute-done.5.refs_3_), channel_id=1, source_target_pairs={{0,8},{4,28},{8,16},{12,4},{16,24},{20,12},{24,0},{28,20},{1,9},{5... | collective-permute-start | bytes 786440 | tf_op jit(solution)/shard_map/ppermute | solution.py:23
  21.8 9.7 %collective-permute-start.8 = (bf16[256,512]{1,0:T(8,128)(2,1)S(1)}, bf16[256,512]{1,0:T(8,128)(2,1)S(1)}, u32[]{:S(2)}, u32[]{:S(2)}) collective-permute-start(bf16[256,512]{1,0:T(8,128)(2,1)S(1)} %collective-permute-done.near.refs_6_), channel_id=1, source_target_pairs={{0,8},{4,28},{8,16},{12,4},{16,24},{20,12},{24,0},{28,20},{1,9},{5... | collective-permute-start | bytes 786440 | tf_op jit(solution)/shard_map/ppermute | solution.py:23
  23.9 6.2 %collective-permute-start.3 = (bf16[3,128,128]{2,1,0:T(8,128)(2,1)S(1)}, bf16[3,128,128]{2,1,0:T(8,128)(2,1)S(1)}, u32[]{:S(2)}, u32[]{:S(2)}) collective-permute-start(bf16[3,128,128]{2,1,0:T(8,128)(2,1)S(1)} %end_blocks.1), channel_id=1, source_target_pairs={{0,4},{4,0},{8,12},{12,8},{16,20},{20,16},{24,28},{28,24},{1,5},{5... | collective-permute-start | bytes 294920 | tf_op jit(solution)/shard_map/ppermute | solution.py:23
  30.7 1.5 %collective-permute-start.7 = (bf16[2,3,128,128]{3,2,1,0:T(8,128)(2,1)S(1)}, bf16[2,3,128,128]{3,2,1,0:T(8,128)(2,1)S(1)}, u32[]{:S(2)}, u32[]{:S(2)}) collective-permute-start(bf16[2,3,128,128]{3,2,1,0:T(8,128)(2,1)S(1)} %get-tuple-element.13), channel_id=1, source_target_pairs={{0,1},{1,0},{2,3},{3,2},{4,5},{5,4},{6,7},{7,6},{8,9},{9,8},{10,11... | collective-permute-start | bytes 589832 | tf_op jit(solution)/shard_map/ppermute | solution.py:23
  32.9 2.7 %collective-permute-start.11 = (bf16[4,3,128,128]{3,2,1,0:T(8,128)(2,1)S(1)}, bf16[4,3,128,128]{3,2,1,0:T(8,128)(2,1)S(1)}, u32[]{:S(2)}, u32[]{:S(2)}) collective-permute-start(bf16[4,3,128,128]{3,2,1,0:T(8,128)(2,1)S(1)} %get-tuple-element.20), channel_id=1, source_target_pairs={{0,1},{1,0},{2,3},{3,2},{4,5},{5,4},{6,7},{7,6},{8,9},{9,8},{10,11... | collective-permute-start | bytes 1179656 | tf_op jit(solution)/shard_map/ppermute | solution.py:23
  33.1 7.8 %collective-permute-start.9 = (bf16[2,3,128,128]{3,2,1,0:T(8,128)(2,1)S(1)}, bf16[2,3,128,128]{3,2,1,0:T(8,128)(2,1)S(1)}, u32[]{:S(2)}, u32[]{:S(2)}) collective-permute-start(bf16[2,3,128,128]{3,2,1,0:T(8,128)(2,1)S(1)} %add.11), channel_id=1, source_target_pairs={{0,2},{1,3},{2,0},{3,1},{4,6},{5,7},{6,4},{7,5},{8,10},{9,11},{10,... | collective-permute-start | bytes 589832 | tf_op jit(solution)/shard_map/ppermute | solution.py:23
  35.4 5.6 %collective-permute-start.10 = (bf16[6,3,128,128]{3,2,1,0:T(8,128)(2,1)S(1)}, bf16[6,3,128,128]{3,2,1,0:T(8,128)(2,1)S(1)}, u32[]{:S(2)}, u32[]{:S(2)}) collective-permute-start(bf16[6,3,128,128]{3,2,1,0:T(8,128)(2,1)S(1)} %get-tuple-element.18), channel_id=1, source_target_pairs={{0,1},{1,0},{2,3},{3,2},{4,5},{5,4},{6,7},{7,6},{8,9},{9,8},{10,11... | collective-permute-start | bytes 1769480 | tf_op jit(solution)/shard_map/ppermute | solution.py:23
  35.6 13.2 %collective-permute-start.12 = (bf16[4,3,128,128]{3,2,1,0:T(8,128)(2,1)S(1)}, bf16[4,3,128,128]{3,2,1,0:T(8,128)(2,1)S(1)}, u32[]{:S(2)}, u32[]{:S(2)}) collective-permute-start(bf16[4,3,128,128]{3,2,1,0:T(8,128)(2,1)S(1)} %add.12), channel_id=1, source_target_pairs={{0,2},{1,3},{2,0},{3,1},{4,6},{5,7},{6,4},{7,5},{8,10},{9,11},{10,... | collective-permute-start | bytes 1179656 | tf_op jit(solution)/shard_map/ppermute | solution.py:23
where the time goes:
time: 49.8 us; the launch traced here: 49.7 us
  starting transfers between devices  21.1 us (42%)
  waiting for transfers between devices  20.6 us (41%)
  Pallas kernels  5.31 us (11%)
  other arithmetic  1.37 us (3%)
  local copies, waits for them, and re-layouts  1.16 us (2%)
    ppermute x13, starting transfers between devices, move(): lax.ppermute(value, axis, [(s, target(s) % count) for s in range(count)])  21.1 us
    ppermute x13, waiting for transfers between devices, move(): lax.ppermute(value, axis, [(s, target(s) % count) for s in range(count)])  20.6 us
    pallas_call x3, Pallas kernels, choose_blocks(): pl.pallas_call(functools.partial(choose_kernel, share, list(pieces), shar...  1.99 us
    pallas_call x1, Pallas kernels, pieces_blocks(): pl.pallas_call(functools.partial(pieces_kernel, list(pieces)), out_shape=...  1.85 us
    reduce_sum x1, other arithmetic, per_device(): jnp.sum(jnp.where(picks, occupation[None, :], jnp.float32(0.0)), axis=1)  1.22 us
    unnamed x10, local copies, waits for them, and re-layouts  1.16 us
  transfers between devices with their start and end apart: 13, of which 7 were waited for; matrix products, arithmetic and copies ran while one was open for 3% of the time, Pallas kernels for 7%

commit v1 on v0

--- a/solution.py
+++ b/solution.py
@@ -162,21 +162,38 @@
     )(near, got)
 
 
+def complete_kernel(chunk, early, got_near, out):
+    start = natural(*chunk)
+    for r in range(early.shape[0]):
+        out[r] = (early[r] + got_near[start + r].astype(jnp.float32)).astype(jnp.bfloat16)
+
+
+def complete(chunk, early, got_near):
+    return pl.pallas_call(
+        functools.partial(complete_kernel, chunk),
+        out_shape=jax.ShapeDtypeStruct(early.shape, got_near.dtype),
+        in_specs=[VMEM] * 2,
+        out_specs=VMEM,
+        compiler_params=pltpu.CompilerParams(vmem_limit_bytes=LIMIT),
+        cost_estimate=SHORT,
+        name="complete",
+    )(early, got_near)
+
+
 def finish_kernel(chunks, early, near, got_near, got, out, rows, done):
     copies = []
 
-    def write(row, total):
-        at = len(copies)
-        rows[at] = total.astype(jnp.bfloat16)
-        copies.append(pltpu.make_async_copy(rows.at[at], out.at[row], done.at[at]))
+    def write(row, rows_of):
+        copies.append(pltpu.make_async_copy(rows_of, out.at[row], done.at[len(copies)]))
         copies[-1].start()
 
     start, later = [natural(*chunk) for chunk in chunks]
     for r in range(early.shape[0]):
-        write(start + r, early[r] + got_near[start + r].astype(jnp.float32))
+        write(start + r, early.at[r])
     for r in range(got.shape[0]):
         total = near[later + r].astype(jnp.float32) + got_near[later + r].astype(jnp.float32)
-        write(later + r, total + got[r].astype(jnp.float32))
+        rows[r] = (total + got[r].astype(jnp.float32)).astype(jnp.bfloat16)
+        write(later + r, rows.at[r])
     for copy in copies:
         copy.wait()
 
@@ -259,7 +276,8 @@
         share, [(1, everyone), (0, everyone)], False, places, scaled, from_partner, scaled, {}, dense
     )
     got_near = move(send, "narrow", lambda n: n ^ 1)
-    return finish(chunks, total(chunks[0], near, sums[0]), near, got_near, sums[1])
+    early = complete(chunks[0], total(chunks[0], near, sums[0]), got_near)
+    return finish(chunks, early, near, got_near, sums[1])
 
 
 def solution(mesh):

time: 49.8 us -> 49.8 us (level)
  transfers between devices with their start and end apart: 13 -> 13, of which waited for: 7 -> 7; matrix products, arithmetic and copies ran while one was open for 3% -> 3% of each run, Pallas kernels for 7% -> 8%
where the time goes in v1:
time: 49.8 us; the launch traced here: 49.7 us
  starting transfers between devices  21.1 us (42%)
  waiting for transfers between devices  20.6 us (41%)
  Pallas kernels  5.35 us (11%)
  other arithmetic  1.37 us (3%)
  local copies, waits for them, and re-layouts  1.16 us (2%)
    ppermute x13, starting transfers between devices, move(): lax.ppermute(value, axis, [(s, target(s) % count) for s in range(count)])  21.1 us
    ppermute x13, waiting for transfers between devices, move(): lax.ppermute(value, axis, [(s, target(s) % count) for s in range(count)])  20.6 us
    pallas_call x3, Pallas kernels, choose_blocks(): pl.pallas_call(functools.partial(choose_kernel, share, list(pieces), shar...  1.99 us
    pallas_call x1, Pallas kernels, pieces_blocks(): pl.pallas_call(functools.partial(pieces_kernel, list(pieces)), out_shape=...  1.85 us
    reduce_sum x1, other arithmetic, per_device(): jnp.sum(jnp.where(picks, occupation[None, :], jnp.float32(0.0)), axis=1)  1.22 us
    unnamed x10, local copies, waits for them, and re-layouts  1.16 us
  transfers between devices with their start and end apart: 13, of which 7 were waited for; matrix products, arithmetic and copies ran while one was open for 3% of the time, Pallas kernels for 8%

profile of v1, /device:TPU:0, one launch (start us, length us, event | category | flops | bytes accessed | tf_op | source)
XLA Modules:
  0.0 49.7 jit_solution(17315888391199077457)
XLA Ops:
  0.0 0.0 copy-start.2
  0.0 0.0 copy-start
  0.0 1.1 %copy-done = bf16[768,512]{1,0:T(8,128)(2,1)S(1)} copy-done((bf16[768,512]{1,0:T(8,128)(2,1)S(1)}, bf16[768,512]{1,0:T(8,128)(2,1)}, u32[]{:S(2)}) %copy-start) | copy-done | bytes 786456
  1.1 0.0 copy-start.3
  1.2 0.0 copy-start.4
  1.2 0.0 copy-start.1
  1.2 3.0 %collective-permute-start.1 = (bf16[256,512]{1,0:T(8,128)(2,1)S(1)}, bf16[256,512]{1,0:T(8,128)(2,1)S(1)}, u32[]{:S(2)}, u32[]{:S(2)}) collective-permute-start(bf16[256,512]{1,0:T(8,128)(2,1)S(1)} %take_end.1.refs_0_), channel_id=1, source_target_pairs={{0,4},{4,0},{8,12},{12,8},{16,20},{20,16},{24,28},{28,24},{1,5},{5... | collective-permute-start | bytes 786440 | tf_op jit(solution)/shard_map/ppermute | solution.py:23
  4.3 0.1 collective-permute-start.5
  4.4 2.1 %collective-permute-start.4 = (bf16[256,512]{1,0:T(8,128)(2,1)S(1)}, bf16[256,512]{1,0:T(8,128)(2,1)S(1)}, u32[]{:S(2)}, u32[]{:S(2)}) collective-permute-start(bf16[256,512]{1,0:T(8,128)(2,1)S(1)} %take_near.2.refs_0_), channel_id=1, source_target_pairs={{0,8},{4,28},{8,16},{12,4},{16,24},{20,12},{24,0},{28,20},{1,9},{5... | collective-permute-start | bytes 786440 | tf_op jit(solution)/shard_map/ppermute | solution.py:23
  6.5 3.6 %collective-permute-start = (bf16[256,512]{1,0:T(8,128)(2,1)S(1)}, bf16[256,512]{1,0:T(8,128)(2,1)S(1)}, u32[]{:S(2)}, u32[]{:S(2)}) collective-permute-start(bf16[256,512]{1,0:T(8,128)(2,1)S(1)} %take_near.3), channel_id=1, source_target_pairs={{0,4},{4,0},{8,12},{12,8},{16,20},{20,16},{24,28},{28,24},{1,5},{5... | collective-permute-start | bytes 786440 | tf_op jit(solution)/shard_map/ppermute | solution.py:23
  10.1 0.0 copy-done.3
  10.1 0.0 copy-done.4
  10.2 1.2 %select_reduce_fusion = f32[512]{0:T(512)S(1)} fusion(f32[4096]{0:T(1024)S(1)} %copy-done.3, s32[512]{0:T(512)S(1)} %copy-done.4), kind=kLoop, calls=%fused_computation | loop fusion | flops 6290944 | bytes 20480 | tf_op jit(solution)/shard_map/reduce_sum | solution.py:245
  11.4 0.0 copy-done.2
  11.4 0.0 collective-permute-done.1.refs_1_
  11.4 2.1 %collective-permute-start.2 = (bf16[256,512]{1,0:T(8,128)(2,1)S(1)}, bf16[256,512]{1,0:T(8,128)(2,1)S(1)}, u32[]{:S(2)}, u32[]{:S(2)}) collective-permute-start(bf16[256,512]{1,0:T(8,128)(2,1)S(1)} %collective-permute-done.1.refs_1_), channel_id=1, source_target_pairs={{0,8},{4,28},{8,16},{12,4},{16,24},{20,12},{24,0},{28,20},{1,9},{5... | collective-permute-start | bytes 786440 | tf_op jit(solution)/shard_map/ppermute | solution.py:23
  13.5 3.5 %collective-permute-done.5.refs_3_ = bf16[256,512]{1,0:T(8,128)(2,1)S(1)} collective-permute-done((bf16[256,512]{1,0:T(8,128)(2,1)S(1)}, bf16[256,512]{1,0:T(8,128)(2,1)S(1)}, u32[]{:S(2)}, u32[]{:S(2)}) %collective-permute-start.5) | collective-permute-done | bytes 262176 | tf_op jit(solution)/shard_map/ppermute | solution.py:23
  17.0 2.1 %collective-permute-start.6 = (bf16[256,512]{1,0:T(8,128)(2,1)S(1)}, bf16[256,512]{1,0:T(8,128)(2,1)S(1)}, u32[]{:S(2)}, u32[]{:S(2)}) collective-permute-start(bf16[256,512]{1,0:T(8,128)(2,1)S(1)} %collective-permute-done.5.refs_3_), channel_id=1, source_target_pairs={{0,8},{4,28},{8,16},{12,4},{16,24},{20,12},{24,0},{28,20},{1,9},{5... | collective-permute-start | bytes 786440 | tf_op jit(solution)/shard_map/ppermute | solution.py:23
  19.1 0.0 copy-done.1
  19.1 0.1 multiply_convert_fusion.left.after
  19.2 2.5 %collective-permute-done.near.refs_6_ = bf16[256,512]{1,0:T(8,128)(2,1)S(1)} collective-permute-done((bf16[256,512]{1,0:T(8,128)(2,1)S(1)}, bf16[256,512]{1,0:T(8,128)(2,1)S(1)}, u32[]{:S(2)}, u32[]{:S(2)}) %collective-permute-start) | collective-permute-done | bytes 262176 | tf_op jit(solution)/shard_map/ppermute | solution.py:23
  21.8 1.8 %collective-permute-start.8 = (bf16[256,512]{1,0:T(8,128)(2,1)S(1)}, bf16[256,512]{1,0:T(8,128)(2,1)S(1)}, u32[]{:S(2)}, u32[]{:S(2)}) collective-permute-start(bf16[256,512]{1,0:T(8,128)(2,1)S(1)} %collective-permute-done.near.refs_6_), channel_id=1, source_target_pairs={{0,8},{4,28},{8,16},{12,4},{16,24},{20,12},{24,0},{28,20},{1,9},{5... | collective-permute-start | bytes 786440 | tf_op jit(solution)/shard_map/ppermute | solution.py:23
  23.6 0.0 collective-permute-done.2.far.refs_4_
  23.6 0.3 end_blocks.1
  23.9 3.6 %collective-permute-start.3 = (bf16[3,128,128]{2,1,0:T(8,128)(2,1)S(1)}, bf16[3,128,128]{2,1,0:T(8,128)(2,1)S(1)}, u32[]{:S(2)}, u32[]{:S(2)}) collective-permute-start(bf16[3,128,128]{2,1,0:T(8,128)(2,1)S(1)} %end_blocks.1), channel_id=1, source_target_pairs={{0,4},{4,0},{8,12},{12,8},{16,20},{20,16},{24,28},{28,24},{1,5},{5... | collective-permute-start | bytes 294920 | tf_op jit(solution)/shard_map/ppermute | solution.py:23
  27.5 0.0 collective-permute-done.4.refs_2_
  27.5 0.0 collective-permute-done.6.refs_5_
  27.5 1.9 %pieces_blocks.1.refs_0_ = bf16[6,22,128,128]{3,2,1,0:T(8,128)(2,1)S(1)} custom-call(bf16[768,512]{1,0:T(8,128)(2,1)S(1)} %multiply_convert_fusion.left.after, bf16[768,512]{1,0:T(8,128)(2,1)S(1)} %copy-done.1, bf16[256,512]{1,0:T(8,128)(2,1)S(1)} %collective-permute-done.1.refs_1_, bf16[256,512]{1,0:T(8,128)(2,1)S(1)} %collective-permute-done.4.refs_2_, ...), custom_call_target="tpu_custom_call" | custom-call | flops 20000000000 | bytes 1 | tf_op jit(solution)/shard_map/pieces_blocks/pallas_call | solution.py:62
  29.3 0.7 %collective-permute-done.3.from_partner = bf16[3,128,128]{2,1,0:T(8,128)(2,1)S(1)} collective-permute-done((bf16[3,128,128]{2,1,0:T(8,128)(2,1)S(1)}, bf16[3,128,128]{2,1,0:T(8,128)(2,1)S(1)}, u32[]{:S(2)}, u32[]{:S(2)}) %collective-permute-start.3) | collective-permute-done | bytes 98336 | tf_op jit(solution)/shard_map/ppermute | solution.py:23
  30.1 0.6 %choose_blocks.3 = (bf16[6,22,128,128]{3,2,1,0:T(8,128)(2,1)S(1)}, bf16[2,3,128,128]{3,2,1,0:T(8,128)(2,1)S(1)}, bf16[2,3,128,128]{3,2,1,0:T(8,128)(2,1)S(1)}) custom-call(s32[6,12]{1,0:T(8,128)S(1)} %add_select_fusion.all_places, bf16[768,512]{1,0:T(8,128)(2,1)S(1)} %multiply_convert_fusion.left.after, ...), custom_call_target="tpu_custom_call", output_to_operand_aliasing={{0}: (4, {})} | custom-call | flops 1 | bytes 1 | tf_op jit(solution)/shard_map/choose_blocks/pallas_call | solution.py:118
  30.7 0.1 collective-permute-start.7
  30.8 0.7 %collective-permute-done.8.refs_0_ = bf16[256,512]{1,0:T(8,128)(2,1)S(1)} collective-permute-done((bf16[256,512]{1,0:T(8,128)(2,1)S(1)}, bf16[256,512]{1,0:T(8,128)(2,1)S(1)}, u32[]{:S(2)}, u32[]{:S(2)}) %collective-permute-start.8) | collective-permute-done | bytes 262176 | tf_op jit(solution)/shard_map/ppermute | solution.py:23
  31.4 0.8 %collective-permute-done.7.after.y = bf16[2,3,128,128]{3,2,1,0:T(8,128)(2,1)S(1)} collective-permute-done((bf16[2,3,128,128]{3,2,1,0:T(8,128)(2,1)S(1)}, bf16[2,3,128,128]{3,2,1,0:T(8,128)(2,1)S(1)}, u32[]{:S(2)}, u32[]{:S(2)}) %collective-permute-start.7) | collective-permute-done | bytes 196640 | tf_op jit(solution)/shard_map/ppermute | solution.py:23
  32.2 0.7 %choose_blocks.4 = (bf16[6,22,128,128]{3,2,1,0:T(8,128)(2,1)S(1)}, bf16[4,3,128,128]{3,2,1,0:T(8,128)(2,1)S(1)}, bf16[4,3,128,128]{3,2,1,0:T(8,128)(2,1)S(1)}) custom-call(s32[6,12]{1,0:T(8,128)S(1)} %add_select_fusion.all_places, bf16[768,512]{1,0:T(8,128)(2,1)S(1)} %multiply_convert_fusion.left.after, ...), custom_call_target="tpu_custom_call", output_to_operand_aliasing={{0}: (5, {})} | custom-call | flops 1 | bytes 1 | tf_op jit(solution)/shard_map/choose_blocks/pallas_call | solution.py:118
  32.9 0.2 collective-permute-start.11
  33.1 1.6 %collective-permute-start.9 = (bf16[2,3,128,128]{3,2,1,0:T(8,128)(2,1)S(1)}, bf16[2,3,128,128]{3,2,1,0:T(8,128)(2,1)S(1)}, u32[]{:S(2)}, u32[]{:S(2)}) collective-permute-start(bf16[2,3,128,128]{3,2,1,0:T(8,128)(2,1)S(1)} %add.11), channel_id=1, source_target_pairs={{0,2},{1,3},{2,0},{3,1},{4,6},{5,7},{6,4},{7,5},{8,10},{9,11},{10,... | collective-permute-start | bytes 589832 | tf_op jit(solution)/shard_map/ppermute | solution.py:23
  34.7 0.7 %choose_blocks.5 = (bf16[6,22,128,128]{3,2,1,0:T(8,128)(2,1)S(1)}, bf16[6,3,128,128]{3,2,1,0:T(8,128)(2,1)S(1)}, bf16[6,3,128,128]{3,2,1,0:T(8,128)(2,1)S(1)}) custom-call(s32[6,12]{1,0:T(8,128)S(1)} %add_select_fusion.all_places, bf16[768,512]{1,0:T(8,128)(2,1)S(1)} %multiply_convert_fusion.left.after, ...), custom_call_target="tpu_custom_call", output_to_operand_aliasing={{0}: (4, {})} | custom-call | flops 1 | bytes 1 | tf_op jit(solution)/shard_map/choose_blocks/pallas_call | solution.py:118
  35.4 0.1 collective-permute-start.10
  35.5 0.0 collective-permute-done.11.y
  35.5 0.1 add.12
  35.6 0.7 %collective-permute-start.12 = (bf16[4,3,128,128]{3,2,1,0:T(8,128)(2,1)S(1)}, bf16[4,3,128,128]{3,2,1,0:T(8,128)(2,1)S(1)}, u32[]{:S(2)}, u32[]{:S(2)}) collective-permute-start(bf16[4,3,128,128]{3,2,1,0:T(8,128)(2,1)S(1)} %add.12), channel_id=1, source_target_pairs={{0,2},{1,3},{2,0},{3,1},{4,6},{5,7},{6,4},{7,5},{8,10},{9,11},{10,... | collective-permute-start | bytes 1179656 | tf_op jit(solution)/shard_map/ppermute | solution.py:23
  36.3 4.6 %collective-permute-done.9.got = bf16[2,3,128,128]{3,2,1,0:T(8,128)(2,1)S(1)} collective-permute-done((bf16[2,3,128,128]{3,2,1,0:T(8,128)(2,1)S(1)}, bf16[2,3,128,128]{3,2,1,0:T(8,128)(2,1)S(1)}, u32[]{:S(2)}, u32[]{:S(2)}) %collective-permute-start.9) | collective-permute-done | bytes 196640 | tf_op jit(solution)/shard_map/ppermute | solution.py:23
  40.9 0.1 total.1.early
  41.0 0.0 collective-permute-done.10.got_near
  41.0 0.1 complete.1.early
  41.1 7.7 %collective-permute-done.12.got = bf16[4,3,128,128]{3,2,1,0:T(8,128)(2,1)S(1)} collective-permute-done((bf16[4,3,128,128]{3,2,1,0:T(8,128)(2,1)S(1)}, bf16[4,3,128,128]{3,2,1,0:T(8,128)(2,1)S(1)}, u32[]{:S(2)}, u32[]{:S(2)}) %collective-permute-start.12) | collective-permute-done | bytes 393248 | tf_op jit(solution)/shard_map/ppermute | solution.py:23
  48.8 0.9 %finish.1 = bf16[6,3,128,128]{3,2,1,0:T(8,128)(2,1)} custom-call(bf16[2,3,128,128]{3,2,1,0:T(8,128)(2,1)S(1)} %complete.1.early, bf16[6,3,128,128]{3,2,1,0:T(8,128)(2,1)S(1)} %get-tuple-element.16.near, bf16[6,3,128,128]{3,2,1,0:T(8,128)(2,1)S(1)} %collective-permute-done.10.got_near, bf16[4,3,128,128]{3,2,1,0:T(8,128)(2,1)S(1)} %collective-permute-done.12.got), custom_call_target="tpu_custom_call" | custom-call | flops 1 | bytes 1 | tf_op jit(solution)/shard_map/finish/pallas_call | solution.py:202
  (7 shorter events, 0.2 us)
Async XLA Ops:
  0.0 11.4 %copy-start.2 = (s32[6,12]{1,0:T(8,128)S(1)}, s32[6,12]{1,0:T(8,128)}, u32[]{:S(2)}) copy-start(s32[6,12]{1,0:T(8,128)} %param.7) | copy-start | bytes 868
  0.0 1.1 %copy-start = (bf16[768,512]{1,0:T(8,128)(2,1)S(1)}, bf16[768,512]{1,0:T(8,128)(2,1)}, u32[]{:S(2)}) copy-start(bf16[768,512]{1,0:T(8,128)(2,1)} %refs_0_.1) | copy-start | bytes 2359300
  1.1 9.0 %copy-start.3 = (f32[4096]{0:T(1024)S(1)}, f32[4096]{0:T(1024)}, u32[]{:S(2)}) copy-start(f32[4096]{0:T(1024)} %param.5) | copy-start | bytes 49156
  1.2 9.0 %copy-start.4 = (s32[512]{0:T(512)S(1)}, s32[512]{0:T(512)}, u32[]{:S(2)}) copy-start(s32[512]{0:T(512)} %param.6) | copy-start | bytes 6148
  1.2 17.9 %copy-start.1 = (bf16[768,512]{1,0:T(8,128)(2,1)S(1)}, bf16[768,512]{1,0:T(8,128)(2,1)}, u32[]{:S(2)}) copy-start(bf16[768,512]{1,0:T(8,128)(2,1)} %refs_0_.1) | copy-start | bytes 2359300
  1.2 10.2 %collective-permute-start.1 = (bf16[256,512]{1,0:T(8,128)(2,1)S(1)}, bf16[256,512]{1,0:T(8,128)(2,1)S(1)}, u32[]{:S(2)}, u32[]{:S(2)}) collective-permute-start(bf16[256,512]{1,0:T(8,128)(2,1)S(1)} %take_end.1.refs_0_), channel_id=1, source_target_pairs={{0,4},{4,0},{8,12},{12,8},{16,20},{20,16},{24,28},{28,24},{1,5},{5... | collective-permute-start | bytes 786440 | tf_op jit(solution)/shard_map/ppermute | solution.py:23
  4.3 12.7 %collective-permute-start.5 = (bf16[256,512]{1,0:T(8,128)(2,1)S(1)}, bf16[256,512]{1,0:T(8,128)(2,1)S(1)}, u32[]{:S(2)}, u32[]{:S(2)}) collective-permute-start(bf16[256,512]{1,0:T(8,128)(2,1)S(1)} %take_middle.1.refs_1_), channel_id=1, source_target_pairs={{0,4},{4,0},{8,12},{12,8},{16,20},{20,16},{24,28},{28,24},{1,5},{5... | collective-permute-start | bytes 786440 | tf_op jit(solution)/shard_map/ppermute | solution.py:23
  4.4 23.1 %collective-permute-start.4 = (bf16[256,512]{1,0:T(8,128)(2,1)S(1)}, bf16[256,512]{1,0:T(8,128)(2,1)S(1)}, u32[]{:S(2)}, u32[]{:S(2)}) collective-permute-start(bf16[256,512]{1,0:T(8,128)(2,1)S(1)} %take_near.2.refs_0_), channel_id=1, source_target_pairs={{0,8},{4,28},{8,16},{12,4},{16,24},{20,12},{24,0},{28,20},{1,9},{5... | collective-permute-start | bytes 786440 | tf_op jit(solution)/shard_map/ppermute | solution.py:23
  6.5 15.2 %collective-permute-start = (bf16[256,512]{1,0:T(8,128)(2,1)S(1)}, bf16[256,512]{1,0:T(8,128)(2,1)S(1)}, u32[]{:S(2)}, u32[]{:S(2)}) collective-permute-start(bf16[256,512]{1,0:T(8,128)(2,1)S(1)} %take_near.3), channel_id=1, source_target_pairs={{0,4},{4,0},{8,12},{12,8},{16,20},{20,16},{24,28},{28,24},{1,5},{5... | collective-permute-start | bytes 786440 | tf_op jit(solution)/shard_map/ppermute | solution.py:23
  11.4 12.2 %collective-permute-start.2 = (bf16[256,512]{1,0:T(8,128)(2,1)S(1)}, bf16[256,512]{1,0:T(8,128)(2,1)S(1)}, u32[]{:S(2)}, u32[]{:S(2)}) collective-permute-start(bf16[256,512]{1,0:T(8,128)(2,1)S(1)} %collective-permute-done.1.refs_1_), channel_id=1, source_target_pairs={{0,8},{4,28},{8,16},{12,4},{16,24},{20,12},{24,0},{28,20},{1,9},{5... | collective-permute-start | bytes 786440 | tf_op jit(solution)/shard_map/ppermute | solution.py:23
  17.0 10.5 %collective-permute-start.6 = (bf16[256,512]{1,0:T(8,128)(2,1)S(1)}, bf16[256,512]{1,0:T(8,128)(2,1)S(1)}, u32[]{:S(2)}, u32[]{:S(2)}) collective-permute-start(bf16[256,512]{1,0:T(8,128)(2,1)S(1)} %collective-permute-done.5.refs_3_), channel_id=1, source_target_pairs={{0,8},{4,28},{8,16},{12,4},{16,24},{20,12},{24,0},{28,20},{1,9},{5... | collective-permute-start | bytes 786440 | tf_op jit(solution)/shard_map/ppermute | solution.py:23
  21.8 9.7 %collective-permute-start.8 = (bf16[256,512]{1,0:T(8,128)(2,1)S(1)}, bf16[256,512]{1,0:T(8,128)(2,1)S(1)}, u32[]{:S(2)}, u32[]{:S(2)}) collective-permute-start(bf16[256,512]{1,0:T(8,128)(2,1)S(1)} %collective-permute-done.near.refs_6_), channel_id=1, source_target_pairs={{0,8},{4,28},{8,16},{12,4},{16,24},{20,12},{24,0},{28,20},{1,9},{5... | collective-permute-start | bytes 786440 | tf_op jit(solution)/shard_map/ppermute | solution.py:23
  23.9 6.2 %collective-permute-start.3 = (bf16[3,128,128]{2,1,0:T(8,128)(2,1)S(1)}, bf16[3,128,128]{2,1,0:T(8,128)(2,1)S(1)}, u32[]{:S(2)}, u32[]{:S(2)}) collective-permute-start(bf16[3,128,128]{2,1,0:T(8,128)(2,1)S(1)} %end_blocks.1), channel_id=1, source_target_pairs={{0,4},{4,0},{8,12},{12,8},{16,20},{20,16},{24,28},{28,24},{1,5},{5... | collective-permute-start | bytes 294920 | tf_op jit(solution)/shard_map/ppermute | solution.py:23
  30.7 1.5 %collective-permute-start.7 = (bf16[2,3,128,128]{3,2,1,0:T(8,128)(2,1)S(1)}, bf16[2,3,128,128]{3,2,1,0:T(8,128)(2,1)S(1)}, u32[]{:S(2)}, u32[]{:S(2)}) collective-permute-start(bf16[2,3,128,128]{3,2,1,0:T(8,128)(2,1)S(1)} %get-tuple-element.13), channel_id=1, source_target_pairs={{0,1},{1,0},{2,3},{3,2},{4,5},{5,4},{6,7},{7,6},{8,9},{9,8},{10,11... | collective-permute-start | bytes 589832 | tf_op jit(solution)/shard_map/ppermute | solution.py:23
  32.9 2.7 %collective-permute-start.11 = (bf16[4,3,128,128]{3,2,1,0:T(8,128)(2,1)S(1)}, bf16[4,3,128,128]{3,2,1,0:T(8,128)(2,1)S(1)}, u32[]{:S(2)}, u32[]{:S(2)}) collective-permute-start(bf16[4,3,128,128]{3,2,1,0:T(8,128)(2,1)S(1)} %get-tuple-element.20), channel_id=1, source_target_pairs={{0,1},{1,0},{2,3},{3,2},{4,5},{5,4},{6,7},{7,6},{8,9},{9,8},{10,11... | collective-permute-start | bytes 1179656 | tf_op jit(solution)/shard_map/ppermute | solution.py:23
  33.1 7.8 %collective-permute-start.9 = (bf16[2,3,128,128]{3,2,1,0:T(8,128)(2,1)S(1)}, bf16[2,3,128,128]{3,2,1,0:T(8,128)(2,1)S(1)}, u32[]{:S(2)}, u32[]{:S(2)}) collective-permute-start(bf16[2,3,128,128]{3,2,1,0:T(8,128)(2,1)S(1)} %add.11), channel_id=1, source_target_pairs={{0,2},{1,3},{2,0},{3,1},{4,6},{5,7},{6,4},{7,5},{8,10},{9,11},{10,... | collective-permute-start | bytes 589832 | tf_op jit(solution)/shard_map/ppermute | solution.py:23
  35.4 5.6 %collective-permute-start.10 = (bf16[6,3,128,128]{3,2,1,0:T(8,128)(2,1)S(1)}, bf16[6,3,128,128]{3,2,1,0:T(8,128)(2,1)S(1)}, u32[]{:S(2)}, u32[]{:S(2)}) collective-permute-start(bf16[6,3,128,128]{3,2,1,0:T(8,128)(2,1)S(1)} %get-tuple-element.18), channel_id=1, source_target_pairs={{0,1},{1,0},{2,3},{3,2},{4,5},{5,4},{6,7},{7,6},{8,9},{9,8},{10,11... | collective-permute-start | bytes 1769480 | tf_op jit(solution)/shard_map/ppermute | solution.py:23
  35.6 13.2 %collective-permute-start.12 = (bf16[4,3,128,128]{3,2,1,0:T(8,128)(2,1)S(1)}, bf16[4,3,128,128]{3,2,1,0:T(8,128)(2,1)S(1)}, u32[]{:S(2)}, u32[]{:S(2)}) collective-permute-start(bf16[4,3,128,128]{3,2,1,0:T(8,128)(2,1)S(1)} %add.12), channel_id=1, source_target_pairs={{0,2},{1,3},{2,0},{3,1},{4,6},{5,7},{6,4},{7,5},{8,10},{9,11},{10,... | collective-permute-start | bytes 1179656 | tf_op jit(solution)/shard_map/ppermute | solution.py:23

commit v2 on v1

--- a/solution.py
+++ b/solution.py
@@ -188,12 +188,12 @@
         copies[-1].start()
 
     start, later = [natural(*chunk) for chunk in chunks]
-    for r in range(early.shape[0]):
-        write(start + r, early.at[r])
+    write(pl.ds(start, early.shape[0]), early)
     for r in range(got.shape[0]):
         total = near[later + r].astype(jnp.float32) + got_near[later + r].astype(jnp.float32)
         rows[r] = (total + got[r].astype(jnp.float32)).astype(jnp.bfloat16)
-        write(later + r, rows.at[r])
+        if r % 2 == 1:
+            write(pl.ds(later + r - 1, 2), rows.at[pl.ds(r - 1, 2)])
     for copy in copies:
         copy.wait()
 

time: 49.8 us -> 49.8 us (level)
  no operation moved by 1% of the time
where the time goes in v2:
time: 49.8 us; the launch traced here: 49.7 us
  starting transfers between devices  21.1 us (42%)
  waiting for transfers between devices  20.6 us (41%)
  Pallas kernels  5.37 us (11%)
  other arithmetic  1.37 us (3%)
  local copies, waits for them, and re-layouts  1.16 us (2%)
    ppermute x13, starting transfers between devices, move(): lax.ppermute(value, axis, [(s, target(s) % count) for s in range(count)])  21.1 us
    ppermute x13, waiting for transfers between devices, move(): lax.ppermute(value, axis, [(s, target(s) % count) for s in range(count)])  20.6 us
    pallas_call x3, Pallas kernels, choose_blocks(): pl.pallas_call(functools.partial(choose_kernel, share, list(pieces), shar...  1.99 us
    pallas_call x1, Pallas kernels, pieces_blocks(): pl.pallas_call(functools.partial(pieces_kernel, list(pieces)), out_shape=...  1.85 us
    reduce_sum x1, other arithmetic, per_device(): jnp.sum(jnp.where(picks, occupation[None, :], jnp.float32(0.0)), axis=1)  1.22 us
    unnamed x10, local copies, waits for them, and re-layouts  1.16 us
  transfers between devices with their start and end apart: 13, of which 7 were waited for; matrix products, arithmetic and copies ran while one was open for 3% of the time, Pallas kernels for 8%

profile of v2, /device:TPU:0, one launch (start us, length us, event | category | flops | bytes accessed | tf_op | source)
XLA Modules:
  0.0 49.7 jit_solution(16475159115978517730)
XLA Ops:
  0.0 0.0 copy-start.2
  0.0 0.0 copy-start
  0.0 1.1 %copy-done = bf16[768,512]{1,0:T(8,128)(2,1)S(1)} copy-done((bf16[768,512]{1,0:T(8,128)(2,1)S(1)}, bf16[768,512]{1,0:T(8,128)(2,1)}, u32[]{:S(2)}) %copy-start) | copy-done | bytes 786456
  1.1 0.0 copy-start.3
  1.2 0.0 copy-start.4
  1.2 0.0 copy-start.1
  1.2 3.0 %collective-permute-start.1 = (bf16[256,512]{1,0:T(8,128)(2,1)S(1)}, bf16[256,512]{1,0:T(8,128)(2,1)S(1)}, u32[]{:S(2)}, u32[]{:S(2)}) collective-permute-start(bf16[256,512]{1,0:T(8,128)(2,1)S(1)} %take_end.1.refs_0_), channel_id=1, source_target_pairs={{0,4},{4,0},{8,12},{12,8},{16,20},{20,16},{24,28},{28,24},{1,5},{5... | collective-permute-start | bytes 786440 | tf_op jit(solution)/shard_map/ppermute | solution.py:23
  4.3 0.1 collective-permute-start.5
  4.4 2.1 %collective-permute-start.4 = (bf16[256,512]{1,0:T(8,128)(2,1)S(1)}, bf16[256,512]{1,0:T(8,128)(2,1)S(1)}, u32[]{:S(2)}, u32[]{:S(2)}) collective-permute-start(bf16[256,512]{1,0:T(8,128)(2,1)S(1)} %take_near.2.refs_0_), channel_id=1, source_target_pairs={{0,8},{4,28},{8,16},{12,4},{16,24},{20,12},{24,0},{28,20},{1,9},{5... | collective-permute-start | bytes 786440 | tf_op jit(solution)/shard_map/ppermute | solution.py:23
  6.5 3.6 %collective-permute-start = (bf16[256,512]{1,0:T(8,128)(2,1)S(1)}, bf16[256,512]{1,0:T(8,128)(2,1)S(1)}, u32[]{:S(2)}, u32[]{:S(2)}) collective-permute-start(bf16[256,512]{1,0:T(8,128)(2,1)S(1)} %take_near.3), channel_id=1, source_target_pairs={{0,4},{4,0},{8,12},{12,8},{16,20},{20,16},{24,28},{28,24},{1,5},{5... | collective-permute-start | bytes 786440 | tf_op jit(solution)/shard_map/ppermute | solution.py:23
  10.1 0.0 copy-done.3
  10.1 0.0 copy-done.4
  10.2 1.2 %select_reduce_fusion = f32[512]{0:T(512)S(1)} fusion(f32[4096]{0:T(1024)S(1)} %copy-done.3, s32[512]{0:T(512)S(1)} %copy-done.4), kind=kLoop, calls=%fused_computation | loop fusion | flops 6290944 | bytes 20480 | tf_op jit(solution)/shard_map/reduce_sum | solution.py:245
  11.4 0.0 copy-done.2
  11.4 0.0 collective-permute-done.1.refs_1_
  11.4 2.1 %collective-permute-start.2 = (bf16[256,512]{1,0:T(8,128)(2,1)S(1)}, bf16[256,512]{1,0:T(8,128)(2,1)S(1)}, u32[]{:S(2)}, u32[]{:S(2)}) collective-permute-start(bf16[256,512]{1,0:T(8,128)(2,1)S(1)} %collective-permute-done.1.refs_1_), channel_id=1, source_target_pairs={{0,8},{4,28},{8,16},{12,4},{16,24},{20,12},{24,0},{28,20},{1,9},{5... | collective-permute-start | bytes 786440 | tf_op jit(solution)/shard_map/ppermute | solution.py:23
  13.5 3.5 %collective-permute-done.5.refs_3_ = bf16[256,512]{1,0:T(8,128)(2,1)S(1)} collective-permute-done((bf16[256,512]{1,0:T(8,128)(2,1)S(1)}, bf16[256,512]{1,0:T(8,128)(2,1)S(1)}, u32[]{:S(2)}, u32[]{:S(2)}) %collective-permute-start.5) | collective-permute-done | bytes 262176 | tf_op jit(solution)/shard_map/ppermute | solution.py:23
  17.0 2.1 %collective-permute-start.6 = (bf16[256,512]{1,0:T(8,128)(2,1)S(1)}, bf16[256,512]{1,0:T(8,128)(2,1)S(1)}, u32[]{:S(2)}, u32[]{:S(2)}) collective-permute-start(bf16[256,512]{1,0:T(8,128)(2,1)S(1)} %collective-permute-done.5.refs_3_), channel_id=1, source_target_pairs={{0,8},{4,28},{8,16},{12,4},{16,24},{20,12},{24,0},{28,20},{1,9},{5... | collective-permute-start | bytes 786440 | tf_op jit(solution)/shard_map/ppermute | solution.py:23
  19.1 0.0 copy-done.1
  19.1 0.1 multiply_convert_fusion.left.after
  19.2 2.5 %collective-permute-done.near.refs_6_ = bf16[256,512]{1,0:T(8,128)(2,1)S(1)} collective-permute-done((bf16[256,512]{1,0:T(8,128)(2,1)S(1)}, bf16[256,512]{1,0:T(8,128)(2,1)S(1)}, u32[]{:S(2)}, u32[]{:S(2)}) %collective-permute-start) | collective-permute-done | bytes 262176 | tf_op jit(solution)/shard_map/ppermute | solution.py:23
  21.8 1.8 %collective-permute-start.8 = (bf16[256,512]{1,0:T(8,128)(2,1)S(1)}, bf16[256,512]{1,0:T(8,128)(2,1)S(1)}, u32[]{:S(2)}, u32[]{:S(2)}) collective-permute-start(bf16[256,512]{1,0:T(8,128)(2,1)S(1)} %collective-permute-done.near.refs_6_), channel_id=1, source_target_pairs={{0,8},{4,28},{8,16},{12,4},{16,24},{20,12},{24,0},{28,20},{1,9},{5... | collective-permute-start | bytes 786440 | tf_op jit(solution)/shard_map/ppermute | solution.py:23
  23.6 0.0 collective-permute-done.2.far.refs_4_
  23.6 0.3 end_blocks.1
  23.9 3.6 %collective-permute-start.3 = (bf16[3,128,128]{2,1,0:T(8,128)(2,1)S(1)}, bf16[3,128,128]{2,1,0:T(8,128)(2,1)S(1)}, u32[]{:S(2)}, u32[]{:S(2)}) collective-permute-start(bf16[3,128,128]{2,1,0:T(8,128)(2,1)S(1)} %end_blocks.1), channel_id=1, source_target_pairs={{0,4},{4,0},{8,12},{12,8},{16,20},{20,16},{24,28},{28,24},{1,5},{5... | collective-permute-start | bytes 294920 | tf_op jit(solution)/shard_map/ppermute | solution.py:23
  27.5 0.0 collective-permute-done.4.refs_2_
  27.5 0.0 collective-permute-done.6.refs_5_
  27.5 1.9 %pieces_blocks.1.refs_0_ = bf16[6,22,128,128]{3,2,1,0:T(8,128)(2,1)S(1)} custom-call(bf16[768,512]{1,0:T(8,128)(2,1)S(1)} %multiply_convert_fusion.left.after, bf16[768,512]{1,0:T(8,128)(2,1)S(1)} %copy-done.1, bf16[256,512]{1,0:T(8,128)(2,1)S(1)} %collective-permute-done.1.refs_1_, bf16[256,512]{1,0:T(8,128)(2,1)S(1)} %collective-permute-done.4.refs_2_, ...), custom_call_target="tpu_custom_call" | custom-call | flops 20000000000 | bytes 1 | tf_op jit(solution)/shard_map/pieces_blocks/pallas_call | solution.py:62
  29.3 0.7 %collective-permute-done.3.from_partner = bf16[3,128,128]{2,1,0:T(8,128)(2,1)S(1)} collective-permute-done((bf16[3,128,128]{2,1,0:T(8,128)(2,1)S(1)}, bf16[3,128,128]{2,1,0:T(8,128)(2,1)S(1)}, u32[]{:S(2)}, u32[]{:S(2)}) %collective-permute-start.3) | collective-permute-done | bytes 98336 | tf_op jit(solution)/shard_map/ppermute | solution.py:23
  30.1 0.6 %choose_blocks.3 = (bf16[6,22,128,128]{3,2,1,0:T(8,128)(2,1)S(1)}, bf16[2,3,128,128]{3,2,1,0:T(8,128)(2,1)S(1)}, bf16[2,3,128,128]{3,2,1,0:T(8,128)(2,1)S(1)}) custom-call(s32[6,12]{1,0:T(8,128)S(1)} %add_select_fusion.all_places, bf16[768,512]{1,0:T(8,128)(2,1)S(1)} %multiply_convert_fusion.left.after, ...), custom_call_target="tpu_custom_call", output_to_operand_aliasing={{0}: (4, {})} | custom-call | flops 1 | bytes 1 | tf_op jit(solution)/shard_map/choose_blocks/pallas_call | solution.py:118
  30.7 0.1 collective-permute-start.7
  30.8 0.7 %collective-permute-done.8.refs_0_ = bf16[256,512]{1,0:T(8,128)(2,1)S(1)} collective-permute-done((bf16[256,512]{1,0:T(8,128)(2,1)S(1)}, bf16[256,512]{1,0:T(8,128)(2,1)S(1)}, u32[]{:S(2)}, u32[]{:S(2)}) %collective-permute-start.8) | collective-permute-done | bytes 262176 | tf_op jit(solution)/shard_map/ppermute | solution.py:23
  31.4 0.8 %collective-permute-done.7.after.y = bf16[2,3,128,128]{3,2,1,0:T(8,128)(2,1)S(1)} collective-permute-done((bf16[2,3,128,128]{3,2,1,0:T(8,128)(2,1)S(1)}, bf16[2,3,128,128]{3,2,1,0:T(8,128)(2,1)S(1)}, u32[]{:S(2)}, u32[]{:S(2)}) %collective-permute-start.7) | collective-permute-done | bytes 196640 | tf_op jit(solution)/shard_map/ppermute | solution.py:23
  32.2 0.7 %choose_blocks.4 = (bf16[6,22,128,128]{3,2,1,0:T(8,128)(2,1)S(1)}, bf16[4,3,128,128]{3,2,1,0:T(8,128)(2,1)S(1)}, bf16[4,3,128,128]{3,2,1,0:T(8,128)(2,1)S(1)}) custom-call(s32[6,12]{1,0:T(8,128)S(1)} %add_select_fusion.all_places, bf16[768,512]{1,0:T(8,128)(2,1)S(1)} %multiply_convert_fusion.left.after, ...), custom_call_target="tpu_custom_call", output_to_operand_aliasing={{0}: (5, {})} | custom-call | flops 1 | bytes 1 | tf_op jit(solution)/shard_map/choose_blocks/pallas_call | solution.py:118
  32.9 0.2 collective-permute-start.11
  33.1 1.6 %collective-permute-start.9 = (bf16[2,3,128,128]{3,2,1,0:T(8,128)(2,1)S(1)}, bf16[2,3,128,128]{3,2,1,0:T(8,128)(2,1)S(1)}, u32[]{:S(2)}, u32[]{:S(2)}) collective-permute-start(bf16[2,3,128,128]{3,2,1,0:T(8,128)(2,1)S(1)} %add.11), channel_id=1, source_target_pairs={{0,2},{1,3},{2,0},{3,1},{4,6},{5,7},{6,4},{7,5},{8,10},{9,11},{10,... | collective-permute-start | bytes 589832 | tf_op jit(solution)/shard_map/ppermute | solution.py:23
  34.7 0.7 %choose_blocks.5 = (bf16[6,22,128,128]{3,2,1,0:T(8,128)(2,1)S(1)}, bf16[6,3,128,128]{3,2,1,0:T(8,128)(2,1)S(1)}, bf16[6,3,128,128]{3,2,1,0:T(8,128)(2,1)S(1)}) custom-call(s32[6,12]{1,0:T(8,128)S(1)} %add_select_fusion.all_places, bf16[768,512]{1,0:T(8,128)(2,1)S(1)} %multiply_convert_fusion.left.after, ...), custom_call_target="tpu_custom_call", output_to_operand_aliasing={{0}: (4, {})} | custom-call | flops 1 | bytes 1 | tf_op jit(solution)/shard_map/choose_blocks/pallas_call | solution.py:118
  35.4 0.1 collective-permute-start.10
  35.5 0.0 collective-permute-done.11.y
  35.5 0.1 add.12
  35.6 0.7 %collective-permute-start.12 = (bf16[4,3,128,128]{3,2,1,0:T(8,128)(2,1)S(1)}, bf16[4,3,128,128]{3,2,1,0:T(8,128)(2,1)S(1)}, u32[]{:S(2)}, u32[]{:S(2)}) collective-permute-start(bf16[4,3,128,128]{3,2,1,0:T(8,128)(2,1)S(1)} %add.12), channel_id=1, source_target_pairs={{0,2},{1,3},{2,0},{3,1},{4,6},{5,7},{6,4},{7,5},{8,10},{9,11},{10,... | collective-permute-start | bytes 1179656 | tf_op jit(solution)/shard_map/ppermute | solution.py:23
  36.3 4.6 %collective-permute-done.9.got = bf16[2,3,128,128]{3,2,1,0:T(8,128)(2,1)S(1)} collective-permute-done((bf16[2,3,128,128]{3,2,1,0:T(8,128)(2,1)S(1)}, bf16[2,3,128,128]{3,2,1,0:T(8,128)(2,1)S(1)}, u32[]{:S(2)}, u32[]{:S(2)}) %collective-permute-start.9) | collective-permute-done | bytes 196640 | tf_op jit(solution)/shard_map/ppermute | solution.py:23
  40.9 0.1 total.1.early
  41.0 0.0 collective-permute-done.10.got_near
  41.0 0.1 complete.1.early
  41.1 7.7 %collective-permute-done.12.got = bf16[4,3,128,128]{3,2,1,0:T(8,128)(2,1)S(1)} collective-permute-done((bf16[4,3,128,128]{3,2,1,0:T(8,128)(2,1)S(1)}, bf16[4,3,128,128]{3,2,1,0:T(8,128)(2,1)S(1)}, u32[]{:S(2)}, u32[]{:S(2)}) %collective-permute-start.12) | collective-permute-done | bytes 393248 | tf_op jit(solution)/shard_map/ppermute | solution.py:23
  48.8 0.9 %finish.1 = bf16[6,3,128,128]{3,2,1,0:T(8,128)(2,1)} custom-call(bf16[2,3,128,128]{3,2,1,0:T(8,128)(2,1)S(1)} %complete.1.early, bf16[6,3,128,128]{3,2,1,0:T(8,128)(2,1)S(1)} %get-tuple-element.16.near, bf16[6,3,128,128]{3,2,1,0:T(8,128)(2,1)S(1)} %collective-permute-done.10.got_near, bf16[4,3,128,128]{3,2,1,0:T(8,128)(2,1)S(1)} %collective-permute-done.12.got), custom_call_target="tpu_custom_call" | custom-call | flops 1 | bytes 1 | tf_op jit(solution)/shard_map/finish/pallas_call | solution.py:202
  (7 shorter events, 0.2 us)
Async XLA Ops:
  0.0 11.4 %copy-start.2 = (s32[6,12]{1,0:T(8,128)S(1)}, s32[6,12]{1,0:T(8,128)}, u32[]{:S(2)}) copy-start(s32[6,12]{1,0:T(8,128)} %param.7) | copy-start | bytes 868
  0.0 1.1 %copy-start = (bf16[768,512]{1,0:T(8,128)(2,1)S(1)}, bf16[768,512]{1,0:T(8,128)(2,1)}, u32[]{:S(2)}) copy-start(bf16[768,512]{1,0:T(8,128)(2,1)} %refs_0_.1) | copy-start | bytes 2359300
  1.1 9.0 %copy-start.3 = (f32[4096]{0:T(1024)S(1)}, f32[4096]{0:T(1024)}, u32[]{:S(2)}) copy-start(f32[4096]{0:T(1024)} %param.5) | copy-start | bytes 49156
  1.2 9.0 %copy-start.4 = (s32[512]{0:T(512)S(1)}, s32[512]{0:T(512)}, u32[]{:S(2)}) copy-start(s32[512]{0:T(512)} %param.6) | copy-start | bytes 6148
  1.2 17.9 %copy-start.1 = (bf16[768,512]{1,0:T(8,128)(2,1)S(1)}, bf16[768,512]{1,0:T(8,128)(2,1)}, u32[]{:S(2)}) copy-start(bf16[768,512]{1,0:T(8,128)(2,1)} %refs_0_.1) | copy-start | bytes 2359300
  1.2 10.2 %collective-permute-start.1 = (bf16[256,512]{1,0:T(8,128)(2,1)S(1)}, bf16[256,512]{1,0:T(8,128)(2,1)S(1)}, u32[]{:S(2)}, u32[]{:S(2)}) collective-permute-start(bf16[256,512]{1,0:T(8,128)(2,1)S(1)} %take_end.1.refs_0_), channel_id=1, source_target_pairs={{0,4},{4,0},{8,12},{12,8},{16,20},{20,16},{24,28},{28,24},{1,5},{5... | collective-permute-start | bytes 786440 | tf_op jit(solution)/shard_map/ppermute | solution.py:23
  4.3 12.7 %collective-permute-start.5 = (bf16[256,512]{1,0:T(8,128)(2,1)S(1)}, bf16[256,512]{1,0:T(8,128)(2,1)S(1)}, u32[]{:S(2)}, u32[]{:S(2)}) collective-permute-start(bf16[256,512]{1,0:T(8,128)(2,1)S(1)} %take_middle.1.refs_1_), channel_id=1, source_target_pairs={{0,4},{4,0},{8,12},{12,8},{16,20},{20,16},{24,28},{28,24},{1,5},{5... | collective-permute-start | bytes 786440 | tf_op jit(solution)/shard_map/ppermute | solution.py:23
  4.4 23.1 %collective-permute-start.4 = (bf16[256,512]{1,0:T(8,128)(2,1)S(1)}, bf16[256,512]{1,0:T(8,128)(2,1)S(1)}, u32[]{:S(2)}, u32[]{:S(2)}) collective-permute-start(bf16[256,512]{1,0:T(8,128)(2,1)S(1)} %take_near.2.refs_0_), channel_id=1, source_target_pairs={{0,8},{4,28},{8,16},{12,4},{16,24},{20,12},{24,0},{28,20},{1,9},{5... | collective-permute-start | bytes 786440 | tf_op jit(solution)/shard_map/ppermute | solution.py:23
  6.5 15.2 %collective-permute-start = (bf16[256,512]{1,0:T(8,128)(2,1)S(1)}, bf16[256,512]{1,0:T(8,128)(2,1)S(1)}, u32[]{:S(2)}, u32[]{:S(2)}) collective-permute-start(bf16[256,512]{1,0:T(8,128)(2,1)S(1)} %take_near.3), channel_id=1, source_target_pairs={{0,4},{4,0},{8,12},{12,8},{16,20},{20,16},{24,28},{28,24},{1,5},{5... | collective-permute-start | bytes 786440 | tf_op jit(solution)/shard_map/ppermute | solution.py:23
  11.4 12.2 %collective-permute-start.2 = (bf16[256,512]{1,0:T(8,128)(2,1)S(1)}, bf16[256,512]{1,0:T(8,128)(2,1)S(1)}, u32[]{:S(2)}, u32[]{:S(2)}) collective-permute-start(bf16[256,512]{1,0:T(8,128)(2,1)S(1)} %collective-permute-done.1.refs_1_), channel_id=1, source_target_pairs={{0,8},{4,28},{8,16},{12,4},{16,24},{20,12},{24,0},{28,20},{1,9},{5... | collective-permute-start | bytes 786440 | tf_op jit(solution)/shard_map/ppermute | solution.py:23
  17.0 10.5 %collective-permute-start.6 = (bf16[256,512]{1,0:T(8,128)(2,1)S(1)}, bf16[256,512]{1,0:T(8,128)(2,1)S(1)}, u32[]{:S(2)}, u32[]{:S(2)}) collective-permute-start(bf16[256,512]{1,0:T(8,128)(2,1)S(1)} %collective-permute-done.5.refs_3_), channel_id=1, source_target_pairs={{0,8},{4,28},{8,16},{12,4},{16,24},{20,12},{24,0},{28,20},{1,9},{5... | collective-permute-start | bytes 786440 | tf_op jit(solution)/shard_map/ppermute | solution.py:23
  21.8 9.7 %collective-permute-start.8 = (bf16[256,512]{1,0:T(8,128)(2,1)S(1)}, bf16[256,512]{1,0:T(8,128)(2,1)S(1)}, u32[]{:S(2)}, u32[]{:S(2)}) collective-permute-start(bf16[256,512]{1,0:T(8,128)(2,1)S(1)} %collective-permute-done.near.refs_6_), channel_id=1, source_target_pairs={{0,8},{4,28},{8,16},{12,4},{16,24},{20,12},{24,0},{28,20},{1,9},{5... | collective-permute-start | bytes 786440 | tf_op jit(solution)/shard_map/ppermute | solution.py:23
  23.9 6.2 %collective-permute-start.3 = (bf16[3,128,128]{2,1,0:T(8,128)(2,1)S(1)}, bf16[3,128,128]{2,1,0:T(8,128)(2,1)S(1)}, u32[]{:S(2)}, u32[]{:S(2)}) collective-permute-start(bf16[3,128,128]{2,1,0:T(8,128)(2,1)S(1)} %end_blocks.1), channel_id=1, source_target_pairs={{0,4},{4,0},{8,12},{12,8},{16,20},{20,16},{24,28},{28,24},{1,5},{5... | collective-permute-start | bytes 294920 | tf_op jit(solution)/shard_map/ppermute | solution.py:23
  30.7 1.5 %collective-permute-start.7 = (bf16[2,3,128,128]{3,2,1,0:T(8,128)(2,1)S(1)}, bf16[2,3,128,128]{3,2,1,0:T(8,128)(2,1)S(1)}, u32[]{:S(2)}, u32[]{:S(2)}) collective-permute-start(bf16[2,3,128,128]{3,2,1,0:T(8,128)(2,1)S(1)} %get-tuple-element.13), channel_id=1, source_target_pairs={{0,1},{1,0},{2,3},{3,2},{4,5},{5,4},{6,7},{7,6},{8,9},{9,8},{10,11... | collective-permute-start | bytes 589832 | tf_op jit(solution)/shard_map/ppermute | solution.py:23
  32.9 2.7 %collective-permute-start.11 = (bf16[4,3,128,128]{3,2,1,0:T(8,128)(2,1)S(1)}, bf16[4,3,128,128]{3,2,1,0:T(8,128)(2,1)S(1)}, u32[]{:S(2)}, u32[]{:S(2)}) collective-permute-start(bf16[4,3,128,128]{3,2,1,0:T(8,128)(2,1)S(1)} %get-tuple-element.20), channel_id=1, source_target_pairs={{0,1},{1,0},{2,3},{3,2},{4,5},{5,4},{6,7},{7,6},{8,9},{9,8},{10,11... | collective-permute-start | bytes 1179656 | tf_op jit(solution)/shard_map/ppermute | solution.py:23
  33.1 7.8 %collective-permute-start.9 = (bf16[2,3,128,128]{3,2,1,0:T(8,128)(2,1)S(1)}, bf16[2,3,128,128]{3,2,1,0:T(8,128)(2,1)S(1)}, u32[]{:S(2)}, u32[]{:S(2)}) collective-permute-start(bf16[2,3,128,128]{3,2,1,0:T(8,128)(2,1)S(1)} %add.11), channel_id=1, source_target_pairs={{0,2},{1,3},{2,0},{3,1},{4,6},{5,7},{6,4},{7,5},{8,10},{9,11},{10,... | collective-permute-start | bytes 589832 | tf_op jit(solution)/shard_map/ppermute | solution.py:23
  35.4 5.6 %collective-permute-start.10 = (bf16[6,3,128,128]{3,2,1,0:T(8,128)(2,1)S(1)}, bf16[6,3,128,128]{3,2,1,0:T(8,128)(2,1)S(1)}, u32[]{:S(2)}, u32[]{:S(2)}) collective-permute-start(bf16[6,3,128,128]{3,2,1,0:T(8,128)(2,1)S(1)} %get-tuple-element.18), channel_id=1, source_target_pairs={{0,1},{1,0},{2,3},{3,2},{4,5},{5,4},{6,7},{7,6},{8,9},{9,8},{10,11... | collective-permute-start | bytes 1769480 | tf_op jit(solution)/shard_map/ppermute | solution.py:23
  35.6 13.2 %collective-permute-start.12 = (bf16[4,3,128,128]{3,2,1,0:T(8,128)(2,1)S(1)}, bf16[4,3,128,128]{3,2,1,0:T(8,128)(2,1)S(1)}, u32[]{:S(2)}, u32[]{:S(2)}) collective-permute-start(bf16[4,3,128,128]{3,2,1,0:T(8,128)(2,1)S(1)} %add.12), channel_id=1, source_target_pairs={{0,2},{1,3},{2,0},{3,1},{4,6},{5,7},{6,4},{7,5},{8,10},{9,11},{10,... | collective-permute-start | bytes 1179656 | tf_op jit(solution)/shard_map/ppermute | solution.py:23
